TPU v7x, 128 devices: a whole 4x4x4 slice. The times are simulated.
128 devices in a mesh: space: 16 (over z, x_lo, core), chaos: 8 (over x_hi, y).
Axes of the slice: x: 4 (x_hi: 2, x_lo: 2; x = x_hi * 2 + x_lo), y: 4, z: 4, core: 2. Of those that a mesh axis runs over, the one named last changes fastest.
Arguments:
- solution: float32 [128, 32, 32, 128], P('chaos', 'space'), may hold values from -6 to 6
- mean_faces: float32 [3, 32, 32, 128], P(None, 'space'), may hold values from 0.5 to 2
- kl_faces: float32 [32, 3, 32, 32, 128], P('chaos', None, 'space'), may hold values from -3 to 3
- multi_index: int32 [128, 32], replicated, may hold values from 0 to 2, as said below
- couplings: int32 [32, 128, 2], replicated, may hold values from 0 to 128, as said below
Outputs:
- applied: float32 [128, 32, 32, 128], P('chaos', 'space')
Inputs may be any that keep to these rules, and one draw needn't show every extreme that they name: `multi_index`: row 0 is the zero multi-index, rows 1 to 32 are the unit multi-indices in order, the other rows are distinct multi-indices of total degree 2 in increasing order of their two variables. couplings[k, i, 0] is the row of multi_index equal to row i plus one in variable k, couplings[k, i, 1] the row equal to row i minus one in variable k, and 128 where no such row exists.
All inputs are finite; a program needn't handle non-finite values.
Results may differ from a plain program's by a relative error of at most 0.00007.
Values sent between devices are 32-bit elements; how exact they have to be, the bound alone decides.
A program may use at most 256 MiB of HBM per device.

v0:
```python
import jax
import jax.numpy as jnp
from jax import lax
from jax.sharding import PartitionSpec as P


def shifted(x, axis, by):
    peers = lax.axis_size(axis)
    pairs = [(i, i + by) for i in range(peers) if 0 <= i + by < peers]
    return lax.ppermute(x, axis, pairs)


def with_halo(block, sides, width):
    for axis, dim in sides:
        count = lax.axis_size(axis)
        forward = [(i, i + 1) for i in range(count - 1)]
        backward = [(target, source) for source, target in forward]
        low = lax.ppermute(
            lax.slice_in_dim(block, block.shape[dim] - width, None, axis=dim), axis, forward
        )
        high = lax.ppermute(lax.slice_in_dim(block, 0, width, axis=dim), axis, backward)
        block = jnp.concatenate([low, block, high], axis=dim)
    return block


def below(face_z, plane):
    return jnp.concatenate([plane[None], face_z[:-1]], axis=0)


def operate_faces(padded, face_x, face_y, face_z, below_z):
    centre = padded[:, 1:-1]
    above = padded[:, 2:]
    beneath = padded[:, :-2]
    next_x = jnp.pad(centre[:, :, 1:], ((0, 0), (0, 0), (0, 1), (0, 0)))
    prev_x = jnp.pad(centre[:, :, :-1], ((0, 0), (0, 0), (1, 0), (0, 0)))
    next_y = jnp.pad(centre[:, :, :, 1:], ((0, 0), (0, 0), (0, 0), (0, 1)))
    prev_y = jnp.pad(centre[:, :, :, :-1], ((0, 0), (0, 0), (0, 0), (1, 0)))
    prior_x = jnp.pad(face_x[:, :-1], ((0, 0), (1, 0), (0, 0)))
    prior_y = jnp.pad(face_y[:, :, :-1], ((0, 0), (0, 0), (1, 0)))
    return (
        face_x * (centre - next_x)
        + prior_x * (centre - prev_x)
        + face_y * (centre - next_y)
        + prior_y * (centre - prev_y)
        + face_z * (centre - above)
        + below_z * (centre - beneath)
    )


def field_apply(mixed, faces, plane):
    return operate_faces(mixed, faces[0], faces[1], faces[2], below(faces[2], plane))


def shards(solution, mean_faces, kl_faces, multi_index, couplings):
    local_modes = solution.shape[0]
    offset = lax.axis_index("chaos") * local_modes
    top_planes = jnp.concatenate([mean_faces[2, -1:], kl_faces[:, 2, -1]], axis=0)
    low_planes = shifted(top_planes, "space", 1)
    whole = lax.all_gather(solution, "chaos", axis=0, tiled=True)
    gathered = with_halo(whole, (("space", 1),), 1)
    total_modes = gathered.shape[0]
    padded_local = lax.dynamic_slice_in_dim(gathered, offset, local_modes, 0)
    result = operate_faces(
        padded_local,
        mean_faces[0],
        mean_faces[1],
        mean_faces[2],
        below(mean_faces[2], low_planes[0]),
    )
    kl_lower = low_planes[1:]
    degrees = lax.dynamic_slice_in_dim(multi_index, offset, local_modes, 0).astype(jnp.float32).T
    partners = lax.dynamic_slice_in_dim(couplings, offset, local_modes, 1)
    up_weight = jnp.where(partners[:, :, 0] < total_modes, jnp.sqrt(degrees + 1.0), 0.0)
    down_weight = jnp.where(partners[:, :, 1] < total_modes, jnp.sqrt(degrees), 0.0)
    mode_ids = jnp.arange(total_modes, dtype=jnp.int32)
    flat_modes = gathered.reshape(total_modes, -1)
    face_piece = lax.all_gather(kl_faces, "chaos", axis=0, tiled=True)
    lower_piece = lax.all_gather(kl_lower, "chaos", axis=0, tiled=True)
    count = face_piece.shape[0]
    selector = up_weight[:, :, None] * (partners[:, :, 0:1] == mode_ids).astype(
        jnp.float32
    ) + down_weight[:, :, None] * (partners[:, :, 1:2] == mode_ids).astype(jnp.float32)
    mixed = jnp.dot(
        selector.reshape(count * local_modes, total_modes),
        flat_modes,
        precision=lax.Precision.HIGHEST,
        preferred_element_type=jnp.float32,
    )
    mixed = mixed.reshape((count, local_modes) + gathered.shape[1:])
    images = jax.vmap(field_apply)(mixed, face_piece, lower_piece)
    return result + jnp.sum(images, axis=0)


def solution(mesh):
    return jax.shard_map(
        shards,
        mesh=mesh,
        in_specs=(
            P("chaos", "space", None, None),
            P(None, "space", None, None),
            P("chaos", None, "space", None, None),
            P(),
            P(),
        ),
        out_specs=P("chaos", "space", None, None),
        check_vma=False,
    )
```

profile of v0, /device:TPU:32, one launch (start us, length us, event | category | flops | bytes accessed | tf_op | source)
XLA Modules:
  0.0 349.1 jit_solution(14645833489202412107)
XLA Ops:
  8.0 75.1 %all-gather.3.cloned.1.call-done = f32[128,2,32,128]{3,2,1,0:T(8,128)} async-done(((f32[16,2,32,128]{3,2,1,0:T(8,128)}), f32[128,2,32,128]{3,2,1,0:T(8,128)}) %all-gather.3.cloned.1.call-update) | async-done | bytes 4194320 | tf_op jit(solution)/shard_map/all_gather | solution.py:59
  83.1 2.7 fusion.24
  85.8 2.5 copy.26
  88.3 1.9 collective-permute-start
  91.1 2.5 copy.27
  93.6 4.5 %collective-permute-start.1 = (f32[128,1,32,128]{3,0,2,1:T(8,128)}, f32[128,1,32,128]{3,0,2,1:T(8,128)}, u32[]{:S(2)}, u32[]{:S(2)}) collective-permute-start(f32[128,1,32,128]{3,0,2,1:T(8,128)} %copy.27), channel_id=1, source_target_pairs={{8,0},{16,8},{24,16},{32,24},{40,32},{48,40},{56,48},{64,56},{72,6... | collective-permute-start | bytes 6291464 | tf_op jit(solution)/shard_map/ppermute | solution.py:21
  98.2 1.9 collective-permute-start.2
  100.5 58.7 %collective-permute-done.2 = f32[5,32,128]{2,1,0:T(8,128)S(1)} collective-permute-done((f32[5,32,128]{2,1,0:T(8,128)S(1)}, f32[5,32,128]{2,1,0:T(8,128)S(1)}, u32[]{:S(2)}, u32[]{:S(2)}) %collective-permute-start.2) | collective-permute-done | bytes 81952 | tf_op jit(solution)/shard_map/ppermute | solution.py:10
  159.2 37.0 %all_gather.11 = f32[32,32,128]{2,1,0:T(8,128)} all-gather(f32[4,32,128]{2,1,0:T(8,128)S(1)} %slice.175), channel_id=1, replica_groups=mesh['space'=16,'chaos'=8] {'chaos'}, dimensions={0}, use_global_device_ids=true | all-gather | bytes 589824 | tf_op jit(solution)/shard_map/all_gather | solution.py:78
  196.3 2.3 slice_bitcast_fusion.2
  198.7 1.1 pad.55
  199.8 1.3 pad.58
  201.1 2.1 pad_maximum_fusion
  203.3 3.1 constant_dynamic-update-slice_fusion.2
  206.4 4.4 %constant_dynamic-update-slice_fusion.1 = f32[128,4,32,128]{3,0,2,1:T(8,128)} fusion(f32[128,4,32,128]{3,0,2,1:T(8,128)} %constant_dynamic-update-slice_fusion.2, f32[128,2,32,128]{3,2,1,0:T(8,128)S(1)} %copy-done), kind=kLoop, calls=%fused_computation.42 | loop fusion | bytes 8388608
  210.8 3.1 constant_dynamic-update-slice_fusion
  214.0 9.0 %copy.20 = f32[128,4,32,128]{0,3,2,1:T(8,128)} copy(f32[128,4,32,128]{3,0,2,1:T(8,128)} %constant_dynamic-update-slice_fusion) | data formatting | bytes 16777216 | tf_op jit(solution)/shard_map/concatenate | solution.py:22
  222.9 32.4 %fusion.5 = f32[32,16,4,32,128]{4,1,3,2,0:T(8,128)} fusion(f32[128,4,32,128]{0,3,2,1:T(8,128)} %copy.20, f32[32,16]{1,0:T(8,128)S(1)} %get-tuple-element.26, s32[32,16]{1,0:T(8,128)S(1)} %bitcast.57, f32[32,16]{1,0:T(8,128)S(1)} %get-tuple-element.25, s32[32,16]{1,0:T(8,128)S(1)} %bitcast.55), kind=kOutput, calls=%fused_computation.7 | convolution fusion | flops 12885229568 | bytes 41951232 | tf_op jit(solution)/shard_map/dot_general | solution.py:83
  255.4 21.7 %fusion.23 = (f32[32,16,2,32,127]{4,1,3,2,0:T(8,128)}, f32[32,16,2,32,127]{4,1,3,2,0:T(8,128)}) fusion(f32[32,16,4,32,128]{4,1,3,2,0:T(8,128)} %fusion.5), kind=kLoop, calls=%fused_computation.52 | loop fusion | bytes 66584576 | tf_op jit(solution)/shard_map/vmap()/slice | solution.py:36
  277.0 21.9 %fusion.22 = (f32[32,16,2,31,128]{4,1,3,2,0:T(8,128)}, f32[32,16,2,31,128]{4,1,3,2,0:T(8,128)}) fusion(f32[32,16,4,32,128]{4,1,3,2,0:T(8,128)} %fusion.5), kind=kLoop, calls=%fused_computation.51 | loop fusion | bytes 65011712 | tf_op jit(solution)/shard_map/vmap()/slice | solution.py:34
  298.9 1.6 constant_dynamic-slice_fusion.4
  300.5 1.5 constant_dynamic-slice_fusion.2
  302.0 37.3 %fusion.2 = f32[16,2,32,128]{3,0,2,1:T(8,128)S(1)} fusion(f32[32,16,4,32,128]{4,1,3,2,0:T(8,128)} %fusion.5, f32[32,16,2,32,127]{4,1,3,2,0:T(8,128)} %get-tuple-element.8, f32[32,16,2,32,127]{4,1,3,2,0:T(8,128)} %get-tuple-element.7, f32[32,16,2,31,128]{4,1,3,2,0:T(8,128)} %get-tuple-element.6, f32[32,16,2,31,128]{4,1,3,2,0:T(8,128)} %get-tuple-element.5, ...), kind=kLoop, calls=%fused_computation.3 | loop fusion | flops 75366400 | bytes 122945536 | tf_op jit(solution)/shard_map/reduce_sum | solution.py:91
  339.3 2.0 fusion.9
  (34 shorter events, 3.7 us)
Async XLA Ops:
  6.5 91.6 %copy-start.4 = (f32[3,2,32,128]{3,2,1,0:T(8,128)S(1)}, f32[3,2,32,128]{3,2,1,0:T(8,128)}, u32[]{:S(2)}) copy-start(f32[3,2,32,128]{3,2,1,0:T(8,128)} %param.6) | copy-start | bytes 294916
  6.5 93.6 %copy-start.5 = (s32[32,128,2]{1,2,0:T(2,128)S(1)}, s32[32,128,2]{1,2,0:T(2,128)}, u32[]{:S(2)}) copy-start(s32[32,128,2]{1,2,0:T(2,128)} %param.9) | copy-start | bytes 98308
  6.5 93.7 %copy-start.6 = (s32[128,32]{0,1:T(8,128)S(1)}, s32[128,32]{0,1:T(8,128)}, u32[]{:S(2)}) copy-start(s32[128,32]{0,1:T(8,128)} %param.8) | copy-start | bytes 49156
  6.5 76.5 %all-gather.3.cloned.1.call-start = ((), (), s32[]{:S(2)}) async-start(), calls=%async_computation | async-start | bytes 4718592 | tf_op jit(solution)/shard_map/all_gather | solution.py:59
  7.3 189.0 %all-gather.5.cloned.1.call-start = ((), (), s32[]{:S(2)}) async-start(), calls=%async_computation.1 | async-start | bytes 3538944 | tf_op jit(solution)/shard_map/all_gather | solution.py:77
  88.3 115.0 %collective-permute-start = (f32[128,1,32,128]{3,0,2,1:T(8,128)}, f32[128,1,32,128]{3,0,2,1:T(8,128)}, u32[]{:S(2)}, u32[]{:S(2)}) collective-permute-start(f32[128,1,32,128]{3,0,2,1:T(8,128)} %copy.26), channel_id=1, source_target_pairs={{0,8},{8,16},{16,24},{24,32},{32,40},{40,48},{48,56},{56,64},{64,7... | collective-permute-start | bytes 6291464 | tf_op jit(solution)/shard_map/ppermute | solution.py:18
  93.6 117.2 %collective-permute-start.1 = (f32[128,1,32,128]{3,0,2,1:T(8,128)}, f32[128,1,32,128]{3,0,2,1:T(8,128)}, u32[]{:S(2)}, u32[]{:S(2)}) collective-permute-start(f32[128,1,32,128]{3,0,2,1:T(8,128)} %copy.27), channel_id=1, source_target_pairs={{8,0},{16,8},{24,16},{32,24},{40,32},{48,40},{56,48},{64,56},{72,6... | collective-permute-start | bytes 6291464 | tf_op jit(solution)/shard_map/ppermute | solution.py:21
  98.2 61.0 %collective-permute-start.2 = (f32[5,32,128]{2,1,0:T(8,128)S(1)}, f32[5,32,128]{2,1,0:T(8,128)S(1)}, u32[]{:S(2)}, u32[]{:S(2)}) collective-permute-start(f32[5,32,128]{2,1,0:T(8,128)S(1)} %pad_maximum_fusion.1), channel_id=1, source_target_pairs={{0,8},{8,16},{16,24},{24,32},{32,40},{40,48},{48,56},{56,64},{64,7... | collective-permute-start | bytes 245768 | tf_op jit(solution)/shard_map/ppermute | solution.py:10
  196.3 10.2 %copy-start = (f32[128,2,32,128]{3,2,1,0:T(8,128)S(1)}, f32[128,2,32,128]{3,2,1,0:T(8,128)}, u32[]{:S(2)}) copy-start(f32[128,2,32,128]{3,2,1,0:T(8,128)} %all-gather.3.cloned.1.call-done) | copy-start | bytes 12582916
  277.0 24.9 %copy-start.1 = (f32[32,2,32,128]{3,2,1,0:T(8,128)S(1)}, f32[32,2,32,128]{3,2,1,0:T(8,128)}, u32[]{:S(2)}) copy-start(f32[32,2,32,128]{3,2,1,0:T(8,128)} %pad.55) | copy-start | bytes 3145732
  277.0 25.0 %copy-start.2 = (f32[32,2,32,128]{3,2,1,0:T(8,128)S(1)}, f32[32,2,32,128]{3,2,1,0:T(8,128)}, u32[]{:S(2)}) copy-start(f32[32,2,32,128]{3,2,1,0:T(8,128)} %pad.58) | copy-start | bytes 3145732
  277.0 25.0 %copy-start.3 = (f32[32,2,32,128]{3,2,1,0:T(8,128)S(1)}, f32[32,2,32,128]{3,2,1,0:T(8,128)}, u32[]{:S(2)}) copy-start(f32[32,2,32,128]{3,2,1,0:T(8,128)} %pad_maximum_fusion) | copy-start | bytes 3145732
Sparse Core Ops, SparseCore 0:
  9.7 73.2 all-gather.2
  85.4 80.2 all-gather.4
where the time goes:
time: 350 us; the launch traced here: 349 us
  waiting for transfers between devices  135 us (39%)
  local copies, waits for them, and re-layouts  80.9 us (23%)
  other arithmetic  41.5 us (12%)
  blocking collectives  37 us (11%)
  matrix products  32.4 us (9%)
  between operations  13.6 us (4%)
  starting transfers between devices  8.41 us (2%)
    all_gather x1, waiting for transfers between devices, shards(): whole = lax.all_gather(solution, 'chaos', axis=0, tiled=True)  75.1 us
    ppermute x1, waiting for transfers between devices, shifted(): return lax.ppermute(x, axis, pairs)  58.7 us
    reduce_sum x1, other arithmetic, shards(): return result + jnp.sum(images, axis=0)  37.3 us
    all_gather x1, blocking collectives, shards(): lower_piece = lax.all_gather(kl_lower, 'chaos', axis=0, tiled=True)  37 us
    dot_general x1, matrix products, shards(): jnp.dot(selector.reshape(count * local_modes, total_modes), flat_modes, p...  32.4 us
    slice x2, local copies, waits for them, and re-layouts, operate_faces(): next_x = jnp.pad(centre[:, :, 1:], ((0, 0), (0, 0), (0, 1), (0, 0)))  23.4 us
    slice x2, local copies, waits for them, and re-layouts, operate_faces(): next_y = jnp.pad(centre[:, :, :, 1:], ((0, 0), (0, 0), (0, 0), (0, 1)))  23.3 us
    unnamed x18, local copies, waits for them, and re-layouts  12.6 us
  transfers between devices with their start and end apart: 5, of which 2 were waited for; matrix products, arithmetic and copies ran while one was open for 7% of the time, Pallas kernels for 0%

commit v1 on v0

v1 whole, which is shorter than its diff:
```python
import math

import jax
import jax.numpy as jnp
from jax import lax
from jax.experimental import pallas as pl
from jax.experimental.pallas import tpu as pltpu
from jax.sharding import PartitionSpec as P

MESH = pl.DeviceIdType.MESH
F32 = jnp.float32
I32 = jnp.int32
SLABS = 16
GROUPS = 8
MODES = 16
FIELDS = 4
KL_TILES = FIELDS * 3 + 3
UNITS = 32
FIRST_PAIR = 33
TOTAL = 128
SLOTS = 192
ROOT2 = math.sqrt(2.0)


def flip_of(slab):
    return lax.rem(lax.div(slab, 4), 2)


def block_of(slab, chaos):
    high = lax.rem(lax.div(chaos, 4) + flip_of(slab), 2)
    y = lax.rem(chaos, 4)
    return high * 4 + high * (3 - y) + (1 - high) * y


def chaos_of(slab, block):
    high = lax.div(block, 4)
    low = lax.rem(block, 4)
    y = high * (3 - low) + (1 - high) * low
    return lax.rem(high + flip_of(slab), 2) * 4 + y


def sublane():
    return lax.broadcasted_iota(I32, (8, 128), 0)


def lane():
    return lax.broadcasted_iota(I32, (8, 128), 1)


def halves(a, b):
    low = sublane() < 4
    return jnp.where(low, a, pltpu.roll(b, 4, 0)), jnp.where(low, pltpu.roll(a, 4, 0), b)


def row(ref_row):
    return jnp.broadcast_to(ref_row, (8, 128))


def make_tables(mi_ref, table_ref):
    shape = (TOTAL, TOTAL)
    mode = lax.broadcasted_iota(I32, shape, 0)
    var = lax.broadcasted_iota(I32, shape, 1)
    degree = jnp.concatenate([mi_ref[...], jnp.zeros((TOTAL - UNITS, TOTAL), I32)], axis=0).T
    is_pair = mode >= FIRST_PAIR
    held = (degree > 0) & is_pair
    count = held.astype(I32)
    running = count
    step = 1
    while step < TOTAL:
        running = running + jnp.where(mode >= step, pltpu.roll(running, step, 0), 0)
        step *= 2
    total = jnp.broadcast_to(running[TOTAL - 1 :, :], (8, TOTAL))
    var8 = lax.broadcasted_iota(I32, (8, TOTAL), 1)
    prefix = total
    step = 1
    while step < UNITS:
        prefix = prefix + jnp.where(var8 >= step, pltpu.roll(prefix, step, 1), 0)
        step *= 2
    start = prefix - total
    place = running - count + jnp.broadcast_to(start[:1, :], shape)
    first = jnp.min(jnp.where(held, var, TOTAL), axis=1, keepdims=True)
    last = jnp.max(jnp.where(held, var, -1), axis=1, keepdims=True)
    place_a = jnp.max(jnp.where(held & (var == first), place, -1), axis=1, keepdims=True)
    place_b = jnp.max(jnp.where(held & (var == last), place, -1), axis=1, keepdims=True)
    column = lax.broadcasted_iota(I32, (TOTAL, 1), 0)
    pair = column >= FIRST_PAIR
    double = first == last
    kind = jnp.where(double, 2, 1)
    first = jnp.where(pair, jnp.minimum(first, UNITS - 1), 0)
    last = jnp.where(pair, jnp.maximum(last, 0), 0)
    code_a = jnp.where(pair, ((column * UNITS + last) * UNITS + first) * 4 + kind, 0)
    code_b = jnp.where(pair & jnp.logical_not(double), ((column * UNITS + first) * UNITS + last) * 4 + kind, 0)
    code_p = (first * UNITS + last) * 4 + kind
    for half in range(2):
        slot = var + half * TOTAL
        code = jnp.where(place_a == slot, code_a, 0) + jnp.where(place_b == slot, code_b, 0)
        table_ref[half] = jnp.broadcast_to(jnp.sum(code, axis=0, keepdims=True), (8, TOTAL))
    table_ref[2] = jnp.broadcast_to(
        jnp.sum(jnp.where(mode == var, code_p, 0), axis=0, keepdims=True), (8, TOTAL)
    )
    table_ref[3] = jnp.where(total > 0, prefix - 1, -1)


def kernel(
    sol_ref, mean_ref, kl_ref, mi_ref, out_ref,
    vsol, vmean, vkl, vmi, send_v, send_k, modes, fields, zface, mean_blocks,
    halo_src_z, halo_src_x, halo_z, halo_x, diff, face, sums, result, table, table_s,
    load_sem, vs_sem, vr_sem, ks_sem, kr_sem, zs_sem, zr_sem, hs_sem, hr_sem, os_sem, or_sem, table_sem,
):
    s, c = lax.axis_index("space"), lax.axis_index("chaos")
    up, down = lax.rem(s + 1, SLABS), lax.rem(s + SLABS - 1, SLABS)
    block = block_of(s, c)
    up_c, down_c = chaos_of(up, block), chaos_of(down, block)
    next_c = chaos_of(s, lax.rem(block + 1, GROUPS))
    prev_c = chaos_of(s, lax.rem(block + GROUPS - 1, GROUPS))

    barrier = pltpu.get_barrier_semaphore()
    peers = [(s, lax.rem(c + d, GROUPS)) for d in range(1, GROUPS)]
    peers += [(up, c), (down, c), (up, up_c), (down, down_c)]
    for peer in peers:
        pl.semaphore_signal(barrier, inc=1, device_id=peer, device_id_type=MESH)

    loads = [
        pltpu.make_async_copy(src, dst, load_sem.at[i])
        for i, (src, dst) in enumerate(((sol_ref, vsol), (kl_ref, vkl), (mean_ref, vmean), (mi_ref, vmi)))
    ]
    for load in loads:
        load.start()

    loads[0].wait()

    @pl.loop(0, MODES)
    def _(i):
        for t in range(4):
            rows = pl.ds(8 * t, 8)
            low, high = halves(vsol[i, 0, rows, :], vsol[i, 1, rows, :])
            send_v[2 * t, i] = low
            send_v[2 * t + 1, i] = high

    pl.semaphore_wait(barrier, len(peers))

    loads[1].wait()
    loads[2].wait()
    z_copies = [
        pltpu.make_async_remote_copy(
            vkl.at[:, 2, 1], zface.at[pl.ds(0, FIELDS)], zs_sem.at[0], zr_sem.at[0], device_id=(up, c), device_id_type=MESH
        ),
        pltpu.make_async_remote_copy(
            vmean.at[2, 1], zface.at[FIELDS], zs_sem.at[1], zr_sem.at[1], device_id=(up, c), device_id_type=MESH
        ),
    ]
    for copy in z_copies:
        copy.start()

    def mode_copy(d):
        target = lax.rem(c + d, GROUPS)
        return pltpu.make_async_remote_copy(
            send_v.at[block_of(s, target)],
            modes.at[pl.ds(c * MODES, MODES)],
            vs_sem.at[d],
            vr_sem.at[c],
            device_id=(s, target),
            device_id_type=MESH,
        )

    for d in range(1, GROUPS):
        mode_copy(d).start()

    @pl.loop(0, MODES)
    def _(i):
        modes[c * MODES + i] = send_v[block, i]

    @pl.loop(0, FIELDS * 3)
    def _(q):
        k, dim = lax.div(q, 3), lax.rem(q, 3)
        for t in range(4):
            rows = pl.ds(8 * t, 8)
            low, high = halves(vkl[k, dim, 0, rows, :], vkl[k, dim, 1, rows, :])
            send_k[2 * t, q] = low
            send_k[2 * t + 1, q] = high

    for b in range(GROUPS):
        for k in range(FIELDS):
            for layer in range(2):
                at = pl.ds(2 * k + layer, 1)
                if b == 0:
                    send_k[b, FIELDS * 3, at, :] = jnp.zeros((1, 128), F32)
                else:
                    send_k[b, FIELDS * 3, at, :] = vkl[k, 0, layer, pl.ds(4 * b - 1, 1), :]

    for copy in z_copies:
        copy.wait()
    for pair in range(2):
        for t in range(4):
            rows = pl.ds(8 * t, 8)
            low, high = halves(zface[2 * pair, rows, :], zface[2 * pair + 1, rows, :])
            send_k[2 * t, FIELDS * 3 + 1 + pair] = low
            send_k[2 * t + 1, FIELDS * 3 + 1 + pair] = high

    def field_copy(d):
        target = lax.rem(c + d, GROUPS)
        return pltpu.make_async_remote_copy(
            send_k.at[block_of(s, target)],
            fields.at[c],
            ks_sem.at[d],
            kr_sem.at[c],
            device_id=(s, target),
            device_id_type=MESH,
        )

    for d in range(1, GROUPS):
        field_copy(d).start()

    @pl.loop(0, KL_TILES)
    def _(q):
        fields[c, q] = send_k[block, q]

    def halo_copies(group):
        cells = pl.ds(group * (MODES // 2), MODES // 2)
        targets = ((up, up_c), (down, down_c), (s, next_c), (s, prev_c))
        copies = []
        for i, target in enumerate(targets):
            source, buffer = (halo_src_z, halo_z) if i < 2 else (halo_src_x, halo_x)
            part = cells if i < 2 else group
            copies.append(
                pltpu.make_async_remote_copy(
                    source.at[i % 2, part],
                    buffer.at[i % 2, part],
                    hs_sem.at[i, group],
                    hr_sem.at[i, group],
                    device_id=target,
                    device_id_type=MESH,
                )
            )
        return copies

    def arrival(d):
        return lax.rem(c + GROUPS - d, GROUPS)

    @pl.loop(0, GROUPS)
    def _(d):
        group = arrival(d)

        @pl.when(d > 0)
        def _():
            pltpu.make_async_copy(send_v.at[0], modes.at[pl.ds(group * MODES, MODES)], vr_sem.at[group]).wait()

        @pl.loop(0, MODES // 2)
        def _(i):
            at = group * (MODES // 2) + i
            low, high = halves(modes[2 * at], modes[2 * at + 1])
            halo_src_z[0, at] = high
            halo_src_z[1, at] = low

        for half in range(2):
            for layer in range(2):
                for i in range(8):
                    m = group * MODES + half * 8 + i
                    at = pl.ds(half * 8 + i, 1)
                    halo_src_x[0, group, layer, at, :] = modes[m, pl.ds(4 * layer + 3, 1), :]
                    halo_src_x[1, group, layer, at, :] = modes[m, pl.ds(4 * layer, 1), :]
        for copy in halo_copies(group):
            copy.start()

    loads[3].wait()
    make_tables(vmi, table)
    to_scalars = pltpu.make_async_copy(table, table_s, table_sem)
    to_scalars.start()

    low4 = sublane() < 4
    sub4 = lax.rem(sublane(), 4)
    below_ok = s > 0
    for t in range(4):
        rows = pl.ds(8 * t, 8)
        parts = [halves(vmean[dim, 0, rows, :], vmean[dim, 1, rows, :]) for dim in range(3)]
        under = zface[FIELDS, rows, :]
        for h in range(2):
            b = 2 * t + h
            fx, fy, fz = (part[h] for part in parts)
            prior = pltpu.roll(fx, 1, 0)
            if b == 0:
                prior = jnp.where(sub4 == 0, 0.0, prior)
            else:
                edges = [row(vmean[0, layer, pl.ds(4 * b - 1, 1), :]) for layer in range(2)]
                prior = jnp.where(sub4 == 0, jnp.where(low4, edges[0], edges[1]), prior)
            lower = under if h == 0 else pltpu.roll(under, 4, 0)
            lower = jnp.where(below_ok, lower, 0.0)
            for q, value in enumerate((fx, prior, fy, fz, jnp.where(low4, lower, pltpu.roll(fz, 4, 0)))):
                mean_blocks[b, q] = value

    above_ok = s < SLABS - 1
    next_ok = block < GROUPS - 1
    last_lane = lane() == 127

    @pl.loop(0, GROUPS)
    def _(d):
        group = arrival(d)
        for copy in halo_copies(group):
            copy.wait_recv()

        @pl.loop(0, MODES // 2)
        def _(i):
            cell = group * (MODES // 2) + i
            under = halo_z[0, cell]
            over = jnp.where(above_ok, halo_z[1, cell], 0.0)
            for odd in range(2):
                m = 2 * cell + odd
                at = pl.ds(2 * i + odd, 1)
                v = modes[m]
                before = jnp.where(low4, row(halo_x[0, group, 0, at, :]), row(halo_x[0, group, 1, at, :]))
                after = jnp.where(low4, row(halo_x[1, group, 0, at, :]), row(halo_x[1, group, 1, at, :]))
                after = jnp.where(next_ok, after, 0.0)
                next_x = jnp.where(sub4 == 3, after, pltpu.roll(v, 7, 0))
                prev_x = jnp.where(sub4 == 0, before, pltpu.roll(v, 1, 0))
                next_y = jnp.where(last_lane, 0.0, pltpu.roll(v, 127, 1))
                swapped = pltpu.roll(v, 4, 0)
                next_z = jnp.where(low4, swapped, over if odd else pltpu.roll(over, 4, 0))
                prev_z = jnp.where(low4, pltpu.roll(under, 4, 0) if odd else under, swapped)
                for q, other in enumerate((next_x, prev_x, next_y, next_z, prev_z)):
                    diff[m, q] = v - other

    @pl.loop(0, GROUPS)
    def _(d):
        group = arrival(d)

        @pl.when(d > 0)
        def _():
            pltpu.make_async_copy(send_k.at[0], fields.at[group], kr_sem.at[group]).wait()

        for k in range(FIELDS):
            fx, fy, fz = (fields[group, 3 * k + dim] for dim in range(3))
            edges = [row(fields[group, FIELDS * 3, pl.ds(2 * k + layer, 1), :]) for layer in range(2)]
            prior = jnp.where(sub4 == 0, jnp.where(low4, edges[0], edges[1]), pltpu.roll(fx, 1, 0))
            under = fields[group, FIELDS * 3 + 1 + k // 2]
            under = under if k % 2 == 0 else pltpu.roll(under, 4, 0)
            lower = jnp.where(low4, jnp.where(below_ok, under, 0.0), pltpu.roll(fz, 4, 0))
            for q, value in enumerate((fx, prior, fy, fz, lower)):
                face[group * FIELDS + k, q] = value

    to_scalars.wait()

    first_lane = lane() == 0

    def term(k, j):
        f, g = [face[k, q] for q in range(5)], [diff[j, q] for q in range(5)]
        return (f[0] * g[0] + f[1] * g[1]) + (f[3] * g[3] + f[4] * g[4]), f[2] * g[2]

    def mean_term(m):
        f, g = [mean_blocks[block, q] for q in range(5)], [diff[m, q] for q in range(5)]
        return (f[0] * g[0] + f[1] * g[1]) + (f[3] * g[3] + f[4] * g[4]), f[2] * g[2]

    def store(m, level, flux):
        result[m] = level + flux - jnp.where(first_lane, 0.0, pltpu.roll(flux, 1, 1))

    @pl.loop(FIRST_PAIR, TOTAL, unroll=5)
    def _(p):
        code = table_s[2, 0, p]
        kind = lax.rem(code, 4)
        b = lax.rem(lax.div(code, 4), UNITS)
        a = lax.div(code, 4 * UNITS)
        weight = jnp.where(kind == 2, F32(0.5 * ROOT2), F32(1.0))
        level, flux = mean_term(p)
        level_a, flux_a = term(a, 1 + b)
        level_b, flux_b = term(b, 1 + a)
        store(p, level + weight * (level_a + level_b), flux + weight * (flux_a + flux_b))

    zero = jnp.zeros((8, 128), F32)

    @pl.loop(0, SLOTS, init_carry=(I32(-1), zero, zero), unroll=4)
    def _(t, carry):
        before, level, flux = carry
        code = table_s[lax.div(t, TOTAL), 0, lax.rem(t, TOTAL)]
        kind = lax.rem(code, 4)
        unit = lax.rem(lax.div(code, 4), UNITS)
        k = lax.rem(lax.div(code, 4 * UNITS), UNITS)
        p = lax.div(code, 4 * UNITS * UNITS)
        weight = jnp.where(kind == 2, F32(ROOT2), jnp.where(kind == 1, F32(1.0), F32(0.0)))
        keep = jnp.where(unit == before, F32(1.0), F32(0.0))
        level_t, flux_t = term(k, p)
        level = keep * level + weight * level_t
        flux = keep * flux + weight * flux_t
        sums[t, 0] = level
        sums[t, 1] = flux
        return unit, level, flux

    @pl.loop(0, UNITS, unroll=4)
    def _(i):
        end = table_s[3, 0, i]
        weight = jnp.where(end >= 0, F32(1.0), F32(0.0))
        end = jnp.maximum(end, 0)
        level, flux = mean_term(1 + i)
        level_0, flux_0 = term(i, 0)
        store(1 + i, level + level_0 + weight * sums[end, 0], flux + flux_0 + weight * sums[end, 1])

    @pl.loop(0, UNITS, init_carry=mean_term(0), unroll=4)
    def total(k, carry):
        level, flux = term(k, 1 + k)
        return carry[0] + level, carry[1] + flux

    store(0, *total)

    def result_copy(d):
        target = lax.rem(c + d, GROUPS)
        return pltpu.make_async_remote_copy(
            result.at[pl.ds(target * MODES, MODES)],
            out_ref.at[block],
            os_sem.at[d],
            or_sem.at[block],
            device_id=(s, target),
            device_id_type=MESH,
        )

    for d in range(1, GROUPS):
        result_copy(d).start()
    own = pltpu.make_async_copy(result.at[pl.ds(c * MODES, MODES)], out_ref.at[block], or_sem.at[block])
    own.start()
    own.wait()
    for d in range(1, GROUPS):
        theirs = block_of(s, arrival(d))
        pltpu.make_async_copy(result.at[pl.ds(0, MODES)], out_ref.at[theirs], or_sem.at[theirs]).wait()
    for d in range(1, GROUPS):
        mode_copy(d).wait_send()
        field_copy(d).wait_send()
        result_copy(d).wait_send()

    @pl.loop(0, GROUPS)
    def _(d):
        for copy in halo_copies(arrival(d)):
            copy.wait_send()


def unpack(blocks_ref, out_ref):
    @pl.loop(0, MODES)
    def _(i):
        for t in range(4):
            rows = pl.ds(8 * t, 8)
            low, high = halves(blocks_ref[2 * t, i], blocks_ref[2 * t + 1, i])
            out_ref[i, 0, rows, :] = low
            out_ref[i, 1, rows, :] = high


def shards(sol, mean, kl, multi_index, couplings):
    tile = (8, 128)
    sem = pltpu.SemaphoreType.DMA
    blocks = pl.pallas_call(
        kernel,
        out_shape=jax.ShapeDtypeStruct((GROUPS, MODES) + tile, F32),
        in_specs=[pl.BlockSpec(memory_space=pltpu.HBM)] * 4,
        out_specs=pl.BlockSpec(memory_space=pl.ANY),
        scratch_shapes=[
            pltpu.VMEM((MODES, 2, 32, 128), F32),
            pltpu.VMEM((3, 2, 32, 128), F32),
            pltpu.VMEM((FIELDS, 3, 2, 32, 128), F32),
            pltpu.VMEM((UNITS, TOTAL), I32),
            pltpu.VMEM((GROUPS, MODES) + tile, F32),
            pltpu.VMEM((GROUPS, KL_TILES) + tile, F32),
            pltpu.VMEM((TOTAL,) + tile, F32),
            pltpu.VMEM((GROUPS, KL_TILES) + tile, F32),
            pltpu.VMEM((FIELDS + 1, 32, 128), F32),
            pltpu.VMEM((GROUPS, 5) + tile, F32),
            pltpu.VMEM((2, TOTAL // 2) + tile, F32),
            pltpu.VMEM((2, GROUPS, 2, MODES, 128), F32),
            pltpu.VMEM((2, TOTAL // 2) + tile, F32),
            pltpu.VMEM((2, GROUPS, 2, MODES, 128), F32),
            pltpu.VMEM((TOTAL, 5) + tile, F32),
            pltpu.VMEM((UNITS, 5) + tile, F32),
            pltpu.VMEM((SLOTS, 2) + tile, F32),
            pltpu.VMEM((TOTAL,) + tile, F32),
            pltpu.VMEM((4,) + tile, I32),
            pltpu.SMEM((4,) + tile, I32),
            sem((4,)),
            sem((GROUPS,)),
            sem((GROUPS,)),
            sem((GROUPS,)),
            sem((GROUPS,)),
            sem((2,)),
            sem((2,)),
            sem((4, GROUPS)),
            sem((4, GROUPS)),
            sem((GROUPS,)),
            sem((GROUPS,)),
            sem,
        ],
        compiler_params=pltpu.CompilerParams(
            collective_id=0, has_side_effects=True, vmem_limit_bytes=60 * 2**20
        ),
        name="apply",
    )(sol, mean, kl, multi_index.T)
    return pl.pallas_call(
        unpack,
        out_shape=jax.ShapeDtypeStruct((MODES, 2, 32, 128), F32),
        in_specs=[pl.BlockSpec(memory_space=pltpu.VMEM)],
        out_specs=pl.BlockSpec(memory_space=pltpu.VMEM),
        name="unpack",
    )(blocks)


def solution(mesh):
    return jax.shard_map(
        shards,
        mesh=mesh,
        in_specs=(
            P("chaos", "space", None, None),
            P(None, "space", None, None),
            P("chaos", None, "space", None, None),
            P(),
            P(),
        ),
        out_specs=P("chaos", "space", None, None),
        check_vma=False,
    )
```

time: 350 us -> 47.5 us (0.14)
  the two profiles are of different devices: /device:TPU:32 before, /device:TPU:24 now
where the time goes in v1:
time: 47.5 us; the launch traced here: 47.3 us
  Pallas kernels  47.3 us (100%)
    pallas_call x1, Pallas kernels, shards(): pl.pallas_call(kernel, out_shape=jax.ShapeDtypeStruct((GROUPS, MODES) + t...  45.3 us
    pallas_call x1, Pallas kernels, shards(): pl.pallas_call(unpack, out_shape=jax.ShapeDtypeStruct((MODES, 2, 32, 128)...  1.96 us

profile of v1, /device:TPU:24, one launch (start us, length us, event | category | flops | bytes accessed | tf_op | source)
XLA Modules:
  0.0 47.3 jit_solution(7477916470101772016)
XLA Ops:
  0.0 45.3 %apply.1.blocks_ref = f32[8,16,8,128]{3,2,1,0:T(8,128)} custom-call(f32[16,2,32,128]{3,2,1,0:T(8,128)} %sol_ref.1, f32[3,2,32,128]{3,2,1,0:T(8,128)} %mean_ref.1, f32[4,3,2,32,128]{4,3,2,1,0:T(8,128)} %kl_ref.1, s32[32,128]{1,0:T(8,128)} %bitcast.1), custom_call_target="tpu_custom_call" | custom-call | tf_op jit(solution)/shard_map/apply/pallas_call | solution.py:445
  45.3 2.0 %unpack.1 = f32[16,2,32,128]{3,2,1,0:T(8,128)} custom-call(f32[8,16,8,128]{3,2,1,0:T(8,128)} %apply.1.blocks_ref), custom_call_target="tpu_custom_call" | custom-call | tf_op jit(solution)/shard_map/unpack/pallas_call | solution.py:489

commit v2 on v1

--- a/solution.py
+++ b/solution.py
@@ -19,6 +19,9 @@
 FIRST_PAIR = 33
 TOTAL = 128
 SLOTS = 192
+PAIR_UNROLL = 19
+SLOT_UNROLL = 16
+UNIT_UNROLL = 8
 ROOT2 = math.sqrt(2.0)
 
 
@@ -88,8 +91,8 @@
     kind = jnp.where(double, 2, 1)
     first = jnp.where(pair, jnp.minimum(first, UNITS - 1), 0)
     last = jnp.where(pair, jnp.maximum(last, 0), 0)
-    code_a = jnp.where(pair, ((column * UNITS + last) * UNITS + first) * 4 + kind, 0)
-    code_b = jnp.where(pair & jnp.logical_not(double), ((column * UNITS + first) * UNITS + last) * 4 + kind, 0)
+    code_a = jnp.where(pair, (column - FIRST_PAIR) * 2 * UNITS + first, 0)
+    code_b = jnp.where(pair & jnp.logical_not(double), ((column - FIRST_PAIR) * 2 + 1) * UNITS + last, 0)
     code_p = (first * UNITS + last) * 4 + kind
     for half in range(2):
         slot = var + half * TOTAL
@@ -104,7 +107,7 @@
 def kernel(
     sol_ref, mean_ref, kl_ref, mi_ref, out_ref,
     vsol, vmean, vkl, vmi, send_v, send_k, modes, fields, zface, mean_blocks,
-    halo_src_z, halo_src_x, halo_z, halo_x, diff, face, sums, result, table, table_s,
+    halo_src_z, halo_src_x, halo_z, halo_x, diff, face, images, sums, result, table, table_s,
     load_sem, vs_sem, vr_sem, ks_sem, kr_sem, zs_sem, zr_sem, hs_sem, hr_sem, os_sem, or_sem, table_sem,
 ):
     s, c = lax.axis_index("space"), lax.axis_index("chaos")
@@ -129,7 +132,7 @@
 
     loads[0].wait()
 
-    @pl.loop(0, MODES)
+    @pl.loop(0, MODES, unroll=4)
     def _(i):
         for t in range(4):
             rows = pl.ds(8 * t, 8)
@@ -166,11 +169,11 @@
     for d in range(1, GROUPS):
         mode_copy(d).start()
 
-    @pl.loop(0, MODES)
+    @pl.loop(0, MODES, unroll=True)
     def _(i):
         modes[c * MODES + i] = send_v[block, i]
 
-    @pl.loop(0, FIELDS * 3)
+    @pl.loop(0, FIELDS * 3, unroll=4)
     def _(q):
         k, dim = lax.div(q, 3), lax.rem(q, 3)
         for t in range(4):
@@ -211,7 +214,7 @@
     for d in range(1, GROUPS):
         field_copy(d).start()
 
-    @pl.loop(0, KL_TILES)
+    @pl.loop(0, KL_TILES, unroll=True)
     def _(q):
         fields[c, q] = send_k[block, q]
 
@@ -245,7 +248,7 @@
         def _():
             pltpu.make_async_copy(send_v.at[0], modes.at[pl.ds(group * MODES, MODES)], vr_sem.at[group]).wait()
 
-        @pl.loop(0, MODES // 2)
+        @pl.loop(0, MODES // 2, unroll=True)
         def _(i):
             at = group * (MODES // 2) + i
             low, high = halves(modes[2 * at], modes[2 * at + 1])
@@ -298,7 +301,7 @@
         for copy in halo_copies(group):
             copy.wait_recv()
 
-        @pl.loop(0, MODES // 2)
+        @pl.loop(0, MODES // 2, unroll=True)
         def _(i):
             cell = group * (MODES // 2) + i
             under = halo_z[0, cell]
@@ -340,64 +343,60 @@
     to_scalars.wait()
 
     first_lane = lane() == 0
-
-    def term(k, j):
-        f, g = [face[k, q] for q in range(5)], [diff[j, q] for q in range(5)]
+    mean = [mean_blocks[block, q] for q in range(5)]
+
+    def planes(ref, at):
+        return [ref[at, q] for q in range(5)]
+
+    def term(f, g):
         return (f[0] * g[0] + f[1] * g[1]) + (f[3] * g[3] + f[4] * g[4]), f[2] * g[2]
 
-    def mean_term(m):
-        f, g = [mean_blocks[block, q] for q in range(5)], [diff[m, q] for q in range(5)]
-        return (f[0] * g[0] + f[1] * g[1]) + (f[3] * g[3] + f[4] * g[4]), f[2] * g[2]
-
-    def store(m, level, flux):
-        result[m] = level + flux - jnp.where(first_lane, 0.0, pltpu.roll(flux, 1, 1))
-
-    @pl.loop(FIRST_PAIR, TOTAL, unroll=5)
+    def gather(level, flux):
+        return level + (flux - jnp.where(first_lane, 0.0, pltpu.roll(flux, 1, 1)))
+
+    @pl.loop(FIRST_PAIR, TOTAL, unroll=PAIR_UNROLL)
     def _(p):
         code = table_s[2, 0, p]
-        kind = lax.rem(code, 4)
-        b = lax.rem(lax.div(code, 4), UNITS)
-        a = lax.div(code, 4 * UNITS)
-        weight = jnp.where(kind == 2, F32(0.5 * ROOT2), F32(1.0))
-        level, flux = mean_term(p)
-        level_a, flux_a = term(a, 1 + b)
-        level_b, flux_b = term(b, 1 + a)
-        store(p, level + weight * (level_a + level_b), flux + weight * (flux_a + flux_b))
+        kind = code & 3
+        b = (code >> 2) & (UNITS - 1)
+        a = code >> 7
+        double = kind == 2
+        weight = jnp.where(double, F32(0.5 * ROOT2), F32(1.0))
+        raised = jnp.where(double, F32(ROOT2), F32(1.0))
+        face_a, face_b, own = planes(face, a), planes(face, b), planes(diff, p)
+        level, flux = term(mean, own)
+        level_a, flux_a = term(face_a, planes(diff, 1 + b))
+        level_b, flux_b = term(face_b, planes(diff, 1 + a))
+        result[p] = gather(level + weight * (level_a + level_b), flux + weight * (flux_a + flux_b))
+        at = 2 * (p - FIRST_PAIR)
+        images[at] = raised * gather(*term(face_b, own))
+        images[at + 1] = raised * gather(*term(face_a, own))
 
     zero = jnp.zeros((8, 128), F32)
 
-    @pl.loop(0, SLOTS, init_carry=(I32(-1), zero, zero), unroll=4)
+    @pl.loop(0, SLOTS, init_carry=(I32(-1), zero), unroll=SLOT_UNROLL)
     def _(t, carry):
-        before, level, flux = carry
-        code = table_s[lax.div(t, TOTAL), 0, lax.rem(t, TOTAL)]
-        kind = lax.rem(code, 4)
-        unit = lax.rem(lax.div(code, 4), UNITS)
-        k = lax.rem(lax.div(code, 4 * UNITS), UNITS)
-        p = lax.div(code, 4 * UNITS * UNITS)
-        weight = jnp.where(kind == 2, F32(ROOT2), jnp.where(kind == 1, F32(1.0), F32(0.0)))
-        keep = jnp.where(unit == before, F32(1.0), F32(0.0))
-        level_t, flux_t = term(k, p)
-        level = keep * level + weight * level_t
-        flux = keep * flux + weight * flux_t
-        sums[t, 0] = level
-        sums[t, 1] = flux
-        return unit, level, flux
-
-    @pl.loop(0, UNITS, unroll=4)
-    def _(i):
+        before, held = carry
+        code = table_s[t >> 7, 0, t & (TOTAL - 1)]
+        unit = code & (UNITS - 1)
+        held = jnp.where(unit == before, held, 0.0) + images[code >> 5]
+        sums[t] = held
+        return unit, held
+
+    zeroth = planes(diff, 0)
+
+    @pl.loop(0, UNITS, init_carry=term(mean, zeroth), unroll=UNIT_UNROLL)
+    def total(i, carry):
         end = table_s[3, 0, i]
         weight = jnp.where(end >= 0, F32(1.0), F32(0.0))
-        end = jnp.maximum(end, 0)
-        level, flux = mean_term(1 + i)
-        level_0, flux_0 = term(i, 0)
-        store(1 + i, level + level_0 + weight * sums[end, 0], flux + flux_0 + weight * sums[end, 1])
-
-    @pl.loop(0, UNITS, init_carry=mean_term(0), unroll=4)
-    def total(k, carry):
-        level, flux = term(k, 1 + k)
-        return carry[0] + level, carry[1] + flux
-
-    store(0, *total)
+        field, own = planes(face, i), planes(diff, 1 + i)
+        level, flux = term(mean, own)
+        level_0, flux_0 = term(field, zeroth)
+        result[1 + i] = gather(level + level_0, flux + flux_0) + weight * sums[jnp.maximum(end, 0)]
+        level_1, flux_1 = term(field, own)
+        return carry[0] + level_1, carry[1] + flux_1
+
+    result[0] = gather(*total)
 
     def result_copy(d):
         target = lax.rem(c + d, GROUPS)
@@ -464,7 +463,8 @@
             pltpu.VMEM((2, GROUPS, 2, MODES, 128), F32),
             pltpu.VMEM((TOTAL, 5) + tile, F32),
             pltpu.VMEM((UNITS, 5) + tile, F32),
-            pltpu.VMEM((SLOTS, 2) + tile, F32),
+            pltpu.VMEM((SLOTS,) + tile, F32),
+            pltpu.VMEM((SLOTS,) + tile, F32),
             pltpu.VMEM((TOTAL,) + tile, F32),
             pltpu.VMEM((4,) + tile, I32),
             pltpu.SMEM((4,) + tile, I32),

time: 47.5 us -> 40.9 us (0.86)
  Pallas kernels: 47.3 us -> 40.7 us
    pallas_call x1, Pallas kernels: 45.3 us -> 38.8 us  [shards(): pl.pallas_call(kernel, out_shape=jax.ShapeDtypeStruct((GROUPS, MODES) + t...]
where the time goes in v2:
time: 40.9 us; the launch traced here: 40.7 us
  Pallas kernels  40.7 us (100%)
    pallas_call x1, Pallas kernels, shards(): pl.pallas_call(kernel, out_shape=jax.ShapeDtypeStruct((GROUPS, MODES) + t...  38.8 us
    pallas_call x1, Pallas kernels, shards(): pl.pallas_call(unpack, out_shape=jax.ShapeDtypeStruct((MODES, 2, 32, 128)...  1.96 us

profile of v2, /device:TPU:24, one launch (start us, length us, event | category | flops | bytes accessed | tf_op | source)
XLA Modules:
  0.0 40.7 jit_solution(10281026061083360265)
XLA Ops:
  0.0 38.8 %apply.1.blocks_ref = f32[8,16,8,128]{3,2,1,0:T(8,128)} custom-call(f32[16,2,32,128]{3,2,1,0:T(8,128)} %sol_ref.1, f32[3,2,32,128]{3,2,1,0:T(8,128)} %mean_ref.1, f32[4,3,2,32,128]{4,3,2,1,0:T(8,128)} %kl_ref.1, s32[32,128]{1,0:T(8,128)} %bitcast.1), custom_call_target="tpu_custom_call" | custom-call | tf_op jit(solution)/shard_map/apply/pallas_call | solution.py:444
  38.8 2.0 %unpack.1 = f32[16,2,32,128]{3,2,1,0:T(8,128)} custom-call(f32[8,16,8,128]{3,2,1,0:T(8,128)} %apply.1.blocks_ref), custom_call_target="tpu_custom_call" | custom-call | tf_op jit(solution)/shard_map/unpack/pallas_call | solution.py:489

commit v3 on v2

--- a/solution.py
+++ b/solution.py
@@ -19,9 +19,11 @@
 FIRST_PAIR = 33
 TOTAL = 128
 SLOTS = 192
-PAIR_UNROLL = 19
-SLOT_UNROLL = 16
-UNIT_UNROLL = 8
+FULL_GROUP = 3
+IMAGE_UNROLL = 95
+SLOT_UNROLL = 48
+RUNS = 4
+UNIT_UNROLL = 32
 ROOT2 = math.sqrt(2.0)
 
 
@@ -40,6 +42,30 @@
     low = lax.rem(block, 4)
     y = high * (3 - low) + (1 - high) * low
     return lax.rem(high + flip_of(slab), 2) * 4 + y
+
+
+def peer_of(chaos, d):
+    high = lax.rem(lax.div(chaos, 4) + lax.div(d, 4), 2)
+    return high * 4 + lax.rem(lax.rem(chaos, 4) + lax.rem(d, 4), 4)
+
+
+def source_of(chaos, d):
+    high = lax.rem(lax.div(chaos, 4) + lax.div(d, 4), 2)
+    return high * 4 + lax.rem(lax.rem(chaos, 4) + 4 - lax.rem(d, 4), 4)
+
+
+def out_peer(chaos, d):
+    d = lax.rem(d, 8)
+    move = d * 0
+    move = move + jnp.where(d == 1, 6, 0)
+    move = move + jnp.where(d == 2, 2, 0)
+    move = move + jnp.where(d == 3, 5, 0)
+    move = move + jnp.where(d == 4, 7, 0)
+    move = move + jnp.where(d == 5, 4, 0)
+    move = move + jnp.where(d == 6, 1, 0)
+    move = move + jnp.where(d == 7, 3, 0)
+    high = lax.rem(lax.div(chaos, 4) + lax.div(move, 4), 2)
+    return high * 4 + lax.rem(lax.rem(chaos, 4) + lax.rem(move, 4), 4)
 
 
 def sublane():
@@ -101,7 +127,12 @@
     table_ref[2] = jnp.broadcast_to(
         jnp.sum(jnp.where(mode == var, code_p, 0), axis=0, keepdims=True), (8, TOTAL)
     )
-    table_ref[3] = jnp.where(total > 0, prefix - 1, -1)
+    end = prefix - 1
+    run = SLOTS // RUNS
+    first_run = sum((start >= r * run).astype(I32) for r in range(1, RUNS))
+    last_run = sum((end >= r * run).astype(I32) for r in range(1, RUNS))
+    table_ref[3] = jnp.where(total > 0, end, SLOTS)
+    table_ref[4] = jnp.where((total > 0) & (last_run > first_run), last_run * run - 1, SLOTS)
 
 
 def kernel(
@@ -140,20 +171,24 @@
             send_v[2 * t, i] = low
             send_v[2 * t + 1, i] = high
 
-    pl.semaphore_wait(barrier, len(peers))
-
-    loads[1].wait()
-    loads[2].wait()
-    z_copies = [
-        pltpu.make_async_remote_copy(
-            vkl.at[:, 2, 1], zface.at[pl.ds(0, FIELDS)], zs_sem.at[0], zr_sem.at[0], device_id=(up, c), device_id_type=MESH
-        ),
-        pltpu.make_async_remote_copy(
-            vmean.at[2, 1], zface.at[FIELDS], zs_sem.at[1], zr_sem.at[1], device_id=(up, c), device_id_type=MESH
-        ),
-    ]
-    for copy in z_copies:
-        copy.start()
+    low4 = sublane() < 4
+    sub4 = lax.rem(sublane(), 4)
+    below_ok = s > 0
+    above_ok = s < SLABS - 1
+    has_next = block < GROUPS - 1
+    has_prev = block > 0
+    last_lane = lane() == 127
+
+    first_lane = lane() == 0
+
+    def planes(ref, at):
+        return [ref[at, q] for q in range(5)]
+
+    def term(f, g):
+        return (f[0] * g[0] + f[1] * g[1]) + (f[3] * g[3] + f[4] * g[4]), f[2] * g[2]
+
+    def gather(level, flux):
+        return level + (flux - jnp.where(first_lane, 0.0, pltpu.roll(flux, 1, 1)))
 
     def mode_copy(d):
         target = lax.rem(c + d, GROUPS)
@@ -166,40 +201,6 @@
             device_id_type=MESH,
         )
 
-    for d in range(1, GROUPS):
-        mode_copy(d).start()
-
-    @pl.loop(0, MODES, unroll=True)
-    def _(i):
-        modes[c * MODES + i] = send_v[block, i]
-
-    @pl.loop(0, FIELDS * 3, unroll=4)
-    def _(q):
-        k, dim = lax.div(q, 3), lax.rem(q, 3)
-        for t in range(4):
-            rows = pl.ds(8 * t, 8)
-            low, high = halves(vkl[k, dim, 0, rows, :], vkl[k, dim, 1, rows, :])
-            send_k[2 * t, q] = low
-            send_k[2 * t + 1, q] = high
-
-    for b in range(GROUPS):
-        for k in range(FIELDS):
-            for layer in range(2):
-                at = pl.ds(2 * k + layer, 1)
-                if b == 0:
-                    send_k[b, FIELDS * 3, at, :] = jnp.zeros((1, 128), F32)
-                else:
-                    send_k[b, FIELDS * 3, at, :] = vkl[k, 0, layer, pl.ds(4 * b - 1, 1), :]
-
-    for copy in z_copies:
-        copy.wait()
-    for pair in range(2):
-        for t in range(4):
-            rows = pl.ds(8 * t, 8)
-            low, high = halves(zface[2 * pair, rows, :], zface[2 * pair + 1, rows, :])
-            send_k[2 * t, FIELDS * 3 + 1 + pair] = low
-            send_k[2 * t + 1, FIELDS * 3 + 1 + pair] = high
-
     def field_copy(d):
         target = lax.rem(c + d, GROUPS)
         return pltpu.make_async_remote_copy(
@@ -211,12 +212,68 @@
             device_id_type=MESH,
         )
 
-    for d in range(1, GROUPS):
-        field_copy(d).start()
-
-    @pl.loop(0, KL_TILES, unroll=True)
-    def _(q):
-        fields[c, q] = send_k[block, q]
+    z_copies = [
+        pltpu.make_async_remote_copy(
+            src, dst, zs_sem.at[i], zr_sem.at[i], device_id=(up, c), device_id_type=MESH
+        )
+        for i, (src, dst) in enumerate(
+            ((vkl.at[:, 2, 1], zface.at[pl.ds(0, FIELDS)]), (vmean.at[2, 1], zface.at[FIELDS]))
+        )
+    ]
+
+    def send_faces_up():
+        loads[2].wait()
+        for copy in z_copies:
+            copy.start()
+
+    def send_modes():
+        for d in range(1, GROUPS):
+            mode_copy(d).start()
+
+    def own_modes():
+        @pl.loop(0, MODES, unroll=True)
+        def _(i):
+            modes[c * MODES + i] = send_v[block, i]
+
+    def pack_fields():
+        loads[1].wait()
+
+        @pl.loop(0, FIELDS * 3, unroll=4)
+        def _(q):
+            k, dim = lax.div(q, 3), lax.rem(q, 3)
+            for t in range(4):
+                rows = pl.ds(8 * t, 8)
+                low, high = halves(vkl[k, dim, 0, rows, :], vkl[k, dim, 1, rows, :])
+                send_k[2 * t, q] = low
+                send_k[2 * t + 1, q] = high
+
+        for b in range(GROUPS):
+            for k in range(FIELDS):
+                for layer in range(2):
+                    at = pl.ds(2 * k + layer, 1)
+                    if b == 0:
+                        send_k[b, FIELDS * 3, at, :] = jnp.zeros((1, 128), F32)
+                    else:
+                        send_k[b, FIELDS * 3, at, :] = vkl[k, 0, layer, pl.ds(4 * b - 1, 1), :]
+
+    def pack_faces_below():
+        for copy in z_copies:
+            copy.wait()
+        for pair in range(2):
+            for t in range(4):
+                rows = pl.ds(8 * t, 8)
+                low, high = halves(zface[2 * pair, rows, :], zface[2 * pair + 1, rows, :])
+                send_k[2 * t, FIELDS * 3 + 1 + pair] = low
+                send_k[2 * t + 1, FIELDS * 3 + 1 + pair] = high
+
+    def send_fields():
+        for d in range(1, GROUPS):
+            field_copy(d).start()
+
+    def own_fields():
+        @pl.loop(0, KL_TILES, unroll=True)
+        def _(q):
+            fields[c, q] = send_k[block, q]
 
     def halo_copies(group):
         cells = pl.ds(group * (MODES // 2), MODES // 2)
@@ -240,14 +297,7 @@
     def arrival(d):
         return lax.rem(c + GROUPS - d, GROUPS)
 
-    @pl.loop(0, GROUPS)
-    def _(d):
-        group = arrival(d)
-
-        @pl.when(d > 0)
-        def _():
-            pltpu.make_async_copy(send_v.at[0], modes.at[pl.ds(group * MODES, MODES)], vr_sem.at[group]).wait()
-
+    def forward(group):
         @pl.loop(0, MODES // 2, unroll=True)
         def _(i):
             at = group * (MODES // 2) + i
@@ -255,51 +305,58 @@
             halo_src_z[0, at] = high
             halo_src_z[1, at] = low
 
-        for half in range(2):
-            for layer in range(2):
-                for i in range(8):
-                    m = group * MODES + half * 8 + i
-                    at = pl.ds(half * 8 + i, 1)
-                    halo_src_x[0, group, layer, at, :] = modes[m, pl.ds(4 * layer + 3, 1), :]
-                    halo_src_x[1, group, layer, at, :] = modes[m, pl.ds(4 * layer, 1), :]
-        for copy in halo_copies(group):
-            copy.start()
-
-    loads[3].wait()
-    make_tables(vmi, table)
+        copies = halo_copies(group)
+        copies[0].start()
+        copies[1].start()
+        for layer in range(2):
+            for i in range(MODES):
+                m = group * MODES + i
+                at = pl.ds(i, 1)
+                halo_src_x[0, group, layer, at, :] = modes[m, pl.ds(4 * layer + 3, 1), :]
+                halo_src_x[1, group, layer, at, :] = modes[m, pl.ds(4 * layer, 1), :]
+        pl.when(has_next)(copies[2].start)
+        pl.when(has_prev)(copies[3].start)
+
+    def forward_arrivals(first, last):
+        @pl.loop(first, last)
+        def _(d):
+            group = arrival(d)
+            pltpu.make_async_copy(send_v.at[0], modes.at[pl.ds(group * MODES, MODES)], vr_sem.at[group]).wait()
+            forward(group)
+
     to_scalars = pltpu.make_async_copy(table, table_s, table_sem)
-    to_scalars.start()
-
-    low4 = sublane() < 4
-    sub4 = lax.rem(sublane(), 4)
-    below_ok = s > 0
-    for t in range(4):
-        rows = pl.ds(8 * t, 8)
-        parts = [halves(vmean[dim, 0, rows, :], vmean[dim, 1, rows, :]) for dim in range(3)]
-        under = zface[FIELDS, rows, :]
-        for h in range(2):
-            b = 2 * t + h
-            fx, fy, fz = (part[h] for part in parts)
-            prior = pltpu.roll(fx, 1, 0)
-            if b == 0:
-                prior = jnp.where(sub4 == 0, 0.0, prior)
-            else:
-                edges = [row(vmean[0, layer, pl.ds(4 * b - 1, 1), :]) for layer in range(2)]
-                prior = jnp.where(sub4 == 0, jnp.where(low4, edges[0], edges[1]), prior)
-            lower = under if h == 0 else pltpu.roll(under, 4, 0)
-            lower = jnp.where(below_ok, lower, 0.0)
-            for q, value in enumerate((fx, prior, fy, fz, jnp.where(low4, lower, pltpu.roll(fz, 4, 0)))):
-                mean_blocks[b, q] = value
-
-    above_ok = s < SLABS - 1
-    next_ok = block < GROUPS - 1
-    last_lane = lane() == 127
-
-    @pl.loop(0, GROUPS)
-    def _(d):
+
+    def tables():
+        loads[3].wait()
+        make_tables(vmi, table)
+        to_scalars.start()
+
+    def mean_faces():
+        for t in range(4):
+            rows = pl.ds(8 * t, 8)
+            parts = [halves(vmean[dim, 0, rows, :], vmean[dim, 1, rows, :]) for dim in range(3)]
+            under = zface[FIELDS, rows, :]
+            for h in range(2):
+                b = 2 * t + h
+                fx, fy, fz = (part[h] for part in parts)
+                prior = pltpu.roll(fx, 1, 0)
+                if b == 0:
+                    prior = jnp.where(sub4 == 0, 0.0, prior)
+                else:
+                    edges = [row(vmean[0, layer, pl.ds(4 * b - 1, 1), :]) for layer in range(2)]
+                    prior = jnp.where(sub4 == 0, jnp.where(low4, edges[0], edges[1]), prior)
+                lower = under if h == 0 else pltpu.roll(under, 4, 0)
+                lower = jnp.where(below_ok, lower, 0.0)
+                for q, value in enumerate((fx, prior, fy, fz, jnp.where(low4, lower, pltpu.roll(fz, 4, 0)))):
+                    mean_blocks[b, q] = value
+
+    def differences(d):
         group = arrival(d)
-        for copy in halo_copies(group):
-            copy.wait_recv()
+        copies = halo_copies(group)
+        copies[0].wait_recv()
+        copies[1].wait_recv()
+        pl.when(has_prev)(copies[2].wait_recv)
+        pl.when(has_next)(copies[3].wait_recv)
 
         @pl.loop(0, MODES // 2, unroll=True)
         def _(i):
@@ -311,25 +368,21 @@
                 at = pl.ds(2 * i + odd, 1)
                 v = modes[m]
                 before = jnp.where(low4, row(halo_x[0, group, 0, at, :]), row(halo_x[0, group, 1, at, :]))
+                before = jnp.where(has_prev, before, 0.0)
                 after = jnp.where(low4, row(halo_x[1, group, 0, at, :]), row(halo_x[1, group, 1, at, :]))
-                after = jnp.where(next_ok, after, 0.0)
+                after = jnp.where(has_next, after, 0.0)
                 next_x = jnp.where(sub4 == 3, after, pltpu.roll(v, 7, 0))
                 prev_x = jnp.where(sub4 == 0, before, pltpu.roll(v, 1, 0))
                 next_y = jnp.where(last_lane, 0.0, pltpu.roll(v, 127, 1))
                 swapped = pltpu.roll(v, 4, 0)
                 next_z = jnp.where(low4, swapped, over if odd else pltpu.roll(over, 4, 0))
                 prev_z = jnp.where(low4, pltpu.roll(under, 4, 0) if odd else under, swapped)
-                for q, other in enumerate((next_x, prev_x, next_y, next_z, prev_z)):
-                    diff[m, q] = v - other
-
-    @pl.loop(0, GROUPS)
-    def _(d):
-        group = arrival(d)
-
-        @pl.when(d > 0)
-        def _():
-            pltpu.make_async_copy(send_k.at[0], fields.at[group], kr_sem.at[group]).wait()
-
+                steps = [v - other for other in (next_x, prev_x, next_y, next_z, prev_z)]
+                for q, value in enumerate(steps):
+                    diff[m, q] = value
+                result[m] = gather(*term(planes(mean_blocks, block), steps))
+
+    def faces(group):
         for k in range(FIELDS):
             fx, fy, fz = (fields[group, 3 * k + dim] for dim in range(3))
             edges = [row(fields[group, FIELDS * 3, pl.ds(2 * k + layer, 1), :]) for layer in range(2)]
@@ -340,92 +393,125 @@
             for q, value in enumerate((fx, prior, fy, fz, lower)):
                 face[group * FIELDS + k, q] = value
 
+    def arrived_faces(first, last):
+        @pl.loop(first, last)
+        def _(d):
+            group = arrival(d)
+            pltpu.make_async_copy(send_k.at[0], fields.at[group], kr_sem.at[group]).wait()
+            faces(group)
+
+    def all_differences(first, last):
+        pl.loop(first, last)(differences)
+
+    pack_fields()
+    own_modes()
+    tables()
+    pl.semaphore_wait(barrier, len(peers))
+    send_faces_up()
+    send_modes()
+    forward(c)
+    pack_faces_below()
+    own_fields()
+    mean_faces()
+    forward_arrivals(1, GROUPS)
+    send_fields()
+    faces(c)
+    all_differences(0, GROUPS)
+    arrived_faces(1, GROUPS)
     to_scalars.wait()
 
-    first_lane = lane() == 0
-    mean = [mean_blocks[block, q] for q in range(5)]
-
-    def planes(ref, at):
-        return [ref[at, q] for q in range(5)]
-
-    def term(f, g):
-        return (f[0] * g[0] + f[1] * g[1]) + (f[3] * g[3] + f[4] * g[4]), f[2] * g[2]
-
-    def gather(level, flux):
-        return level + (flux - jnp.where(first_lane, 0.0, pltpu.roll(flux, 1, 1)))
-
-    @pl.loop(FIRST_PAIR, TOTAL, unroll=PAIR_UNROLL)
-    def _(p):
-        code = table_s[2, 0, p]
-        kind = code & 3
-        b = (code >> 2) & (UNITS - 1)
-        a = code >> 7
-        double = kind == 2
-        weight = jnp.where(double, F32(0.5 * ROOT2), F32(1.0))
-        raised = jnp.where(double, F32(ROOT2), F32(1.0))
-        face_a, face_b, own = planes(face, a), planes(face, b), planes(diff, p)
-        level, flux = term(mean, own)
-        level_a, flux_a = term(face_a, planes(diff, 1 + b))
-        level_b, flux_b = term(face_b, planes(diff, 1 + a))
-        result[p] = gather(level + weight * (level_a + level_b), flux + weight * (flux_a + flux_b))
-        at = 2 * (p - FIRST_PAIR)
-        images[at] = raised * gather(*term(face_b, own))
-        images[at + 1] = raised * gather(*term(face_a, own))
-
-    zero = jnp.zeros((8, 128), F32)
-
-    @pl.loop(0, SLOTS, init_carry=(I32(-1), zero), unroll=SLOT_UNROLL)
-    def _(t, carry):
-        before, held = carry
-        code = table_s[t >> 7, 0, t & (TOTAL - 1)]
-        unit = code & (UNITS - 1)
-        held = jnp.where(unit == before, held, 0.0) + images[code >> 5]
-        sums[t] = held
-        return unit, held
-
-    zeroth = planes(diff, 0)
-
-    @pl.loop(0, UNITS, init_carry=term(mean, zeroth), unroll=UNIT_UNROLL)
-    def total(i, carry):
-        end = table_s[3, 0, i]
-        weight = jnp.where(end >= 0, F32(1.0), F32(0.0))
-        field, own = planes(face, i), planes(diff, 1 + i)
-        level, flux = term(mean, own)
-        level_0, flux_0 = term(field, zeroth)
-        result[1 + i] = gather(level + level_0, flux + flux_0) + weight * sums[jnp.maximum(end, 0)]
-        level_1, flux_1 = term(field, own)
-        return carry[0] + level_1, carry[1] + flux_1
-
-    result[0] = gather(*total)
-
-    def result_copy(d):
-        target = lax.rem(c + d, GROUPS)
+    def result_copy(target):
         return pltpu.make_async_remote_copy(
             result.at[pl.ds(target * MODES, MODES)],
             out_ref.at[block],
-            os_sem.at[d],
+            os_sem.at[target],
             or_sem.at[block],
             device_id=(s, target),
             device_id_type=MESH,
         )
 
-    for d in range(1, GROUPS):
-        result_copy(d).start()
-    own = pltpu.make_async_copy(result.at[pl.ds(c * MODES, MODES)], out_ref.at[block], or_sem.at[block])
-    own.start()
-    own.wait()
-    for d in range(1, GROUPS):
-        theirs = block_of(s, arrival(d))
-        pltpu.make_async_copy(result.at[pl.ds(0, MODES)], out_ref.at[theirs], or_sem.at[theirs]).wait()
+    def send_result(target):
+        pl.when(target != c)(lambda: result_copy(target).start())
+        own = pltpu.make_async_copy(result.at[pl.ds(target * MODES, MODES)], out_ref.at[block], or_sem.at[block])
+        pl.when(target == c)(own.start)
+
+    def variables(p):
+        code = table_s[2, 0, p]
+        return code >> 7, (code >> 2) & (UNITS - 1), (code & 3) == 2
+
+    def image(p):
+        a, b, double = variables(p)
+        raised = jnp.where(double, F32(ROOT2), F32(1.0))
+        own = planes(diff, p)
+        at = 2 * (p - FIRST_PAIR)
+        images[at] = raised * gather(*term(planes(face, b), own))
+        images[at + 1] = raised * gather(*term(planes(face, a), own))
+
+    def pair(p):
+        a, b, double = variables(p)
+        weight = jnp.where(double, F32(0.5 * ROOT2), F32(1.0))
+        level_a, flux_a = term(planes(face, a), planes(diff, 1 + b))
+        level_b, flux_b = term(planes(face, b), planes(diff, 1 + a))
+        result[p] = result[p] + weight * gather(level_a + level_b, flux_a + flux_b)
+
+    pl.loop(FIRST_PAIR, TOTAL, unroll=IMAGE_UNROLL)(image)
+
+    zero = jnp.zeros((8, 128), F32)
+    sums[SLOTS] = zero
+    run = SLOTS // RUNS
+
+    @pl.loop(0, run, init_carry=((I32(-1), zero),) * RUNS, unroll=SLOT_UNROLL)
+    def _(t, carry):
+        now = []
+        for r, (before, held) in enumerate(carry):
+            at = t + r * run
+            code = table_s[at >> 7, 0, at & (TOTAL - 1)]
+            unit = code & (UNITS - 1)
+            held = jnp.where(unit == before, held, 0.0) + images[code >> 5]
+            sums[at] = held
+            now.append((unit, held))
+        return tuple(now)
+
+    zeroth = planes(diff, 0)
+
+    @pl.loop(0, UNITS, init_carry=(zero, zero), unroll=UNIT_UNROLL)
+    def total(i, carry):
+        field = planes(face, i)
+        partial = sums[table_s[3, 0, i]] + sums[table_s[4, 0, i]]
+        result[1 + i] = result[1 + i] + gather(*term(field, zeroth)) + partial
+        level, flux = term(field, planes(diff, 1 + i))
+        return carry[0] + level, carry[1] + flux
+
+    result[0] = result[0] + gather(*total)
+
+    pl.loop(FIRST_PAIR, FULL_GROUP * MODES, unroll=True)(pair)
+
+    @pl.loop(1, GROUPS + 1)
+    def _(d):
+        target = out_peer(c, d)
+
+        @pl.when(target >= FULL_GROUP)
+        def _():
+            @pl.loop(0, MODES, unroll=True)
+            def _(i):
+                pair(target * MODES + i)
+
+        send_result(target)
+
+    for b in range(GROUPS):
+        pltpu.make_async_copy(result.at[pl.ds(0, MODES)], out_ref.at[b], or_sem.at[b]).wait()
     for d in range(1, GROUPS):
         mode_copy(d).wait_send()
         field_copy(d).wait_send()
-        result_copy(d).wait_send()
+        result_copy(peer_of(c, d)).wait_send()
 
     @pl.loop(0, GROUPS)
     def _(d):
-        for copy in halo_copies(arrival(d)):
-            copy.wait_send()
+        copies = halo_copies(arrival(d))
+        copies[0].wait_send()
+        copies[1].wait_send()
+        pl.when(has_next)(copies[2].wait_send)
+        pl.when(has_prev)(copies[3].wait_send)
 
 
 def unpack(blocks_ref, out_ref):
@@ -464,10 +550,10 @@
             pltpu.VMEM((TOTAL, 5) + tile, F32),
             pltpu.VMEM((UNITS, 5) + tile, F32),
             pltpu.VMEM((SLOTS,) + tile, F32),
-            pltpu.VMEM((SLOTS,) + tile, F32),
+            pltpu.VMEM((SLOTS + 1,) + tile, F32),
             pltpu.VMEM((TOTAL,) + tile, F32),
-            pltpu.VMEM((4,) + tile, I32),
-            pltpu.SMEM((4,) + tile, I32),
+            pltpu.VMEM((5,) + tile, I32),
+            pltpu.SMEM((5,) + tile, I32),
             sem((4,)),
             sem((GROUPS,)),
             sem((GROUPS,)),

time: 40.9 us -> 37.8 us (0.924)
  the two profiles are of different devices: /device:TPU:24 before, /device:TPU:32 now
where the time goes in v3:
time: 37.8 us; the launch traced here: 37.6 us
  Pallas kernels  37.6 us (99%)
    pallas_call x1, Pallas kernels, shards(): pl.pallas_call(kernel, out_shape=jax.ShapeDtypeStruct((GROUPS, MODES) + t...  35.7 us
    pallas_call x1, Pallas kernels, shards(): pl.pallas_call(unpack, out_shape=jax.ShapeDtypeStruct((MODES, 2, 32, 128)...  1.96 us

profile of v3, /device:TPU:32, one launch (start us, length us, event | category | flops | bytes accessed | tf_op | source)
XLA Modules:
  0.0 37.6 jit_solution(82943057666430374)
XLA Ops:
  0.0 35.7 %apply.1.blocks_ref = f32[8,16,8,128]{3,2,1,0:T(8,128)} custom-call(f32[16,2,32,128]{3,2,1,0:T(8,128)} %sol_ref.1, f32[3,2,32,128]{3,2,1,0:T(8,128)} %mean_ref.1, f32[4,3,2,32,128]{4,3,2,1,0:T(8,128)} %kl_ref.1, s32[32,128]{1,0:T(8,128)} %bitcast.1), custom_call_target="tpu_custom_call" | custom-call | tf_op jit(solution)/shard_map/apply/pallas_call | solution.py:530
  35.7 2.0 %unpack.1 = f32[16,2,32,128]{3,2,1,0:T(8,128)} custom-call(f32[8,16,8,128]{3,2,1,0:T(8,128)} %apply.1.blocks_ref), custom_call_target="tpu_custom_call" | custom-call | tf_op jit(solution)/shard_map/unpack/pallas_call | solution.py:575

commit v4 on v3

--- a/solution.py
+++ b/solution.py
@@ -33,14 +33,14 @@
 
 def block_of(slab, chaos):
     high = lax.rem(lax.div(chaos, 4) + flip_of(slab), 2)
-    y = lax.rem(chaos, 4)
+    y = lax.rem(lax.rem(chaos, 4) + 1, 4)
     return high * 4 + high * (3 - y) + (1 - high) * y
 
 
 def chaos_of(slab, block):
     high = lax.div(block, 4)
     low = lax.rem(block, 4)
-    y = high * (3 - low) + (1 - high) * low
+    y = lax.rem(high * (3 - low) + (1 - high) * low + 3, 4)
     return lax.rem(high + flip_of(slab), 2) * 4 + y
 
 
@@ -66,6 +66,34 @@
     move = move + jnp.where(d == 7, 3, 0)
     high = lax.rem(lax.div(chaos, 4) + lax.div(move, 4), 2)
     return high * 4 + lax.rem(lax.rem(chaos, 4) + lax.rem(move, 4), 4)
+
+
+def in_peer(chaos, d):
+    d = lax.rem(d, 8)
+    move = d * 0
+    move = move + jnp.where(d == 1, 6, 0)
+    move = move + jnp.where(d == 2, 2, 0)
+    move = move + jnp.where(d == 3, 5, 0)
+    move = move + jnp.where(d == 4, 7, 0)
+    move = move + jnp.where(d == 5, 4, 0)
+    move = move + jnp.where(d == 6, 1, 0)
+    move = move + jnp.where(d == 7, 3, 0)
+    high = lax.rem(lax.div(chaos, 4) + lax.div(move, 4), 2)
+    return high * 4 + lax.rem(lax.rem(chaos, 4) + lax.rem(move, 4), 4)
+
+
+def in_source(chaos, d):
+    d = lax.rem(d, 8)
+    move = d * 0
+    move = move + jnp.where(d == 1, 6, 0)
+    move = move + jnp.where(d == 2, 2, 0)
+    move = move + jnp.where(d == 3, 5, 0)
+    move = move + jnp.where(d == 4, 7, 0)
+    move = move + jnp.where(d == 5, 4, 0)
+    move = move + jnp.where(d == 6, 1, 0)
+    move = move + jnp.where(d == 7, 3, 0)
+    high = lax.rem(lax.div(chaos, 4) + lax.div(move, 4), 2)
+    return high * 4 + lax.rem(lax.rem(chaos, 4) + 4 - lax.rem(move, 4), 4)
 
 
 def sublane():
@@ -191,7 +219,7 @@
         return level + (flux - jnp.where(first_lane, 0.0, pltpu.roll(flux, 1, 1)))
 
     def mode_copy(d):
-        target = lax.rem(c + d, GROUPS)
+        target = in_peer(c, d)
         return pltpu.make_async_remote_copy(
             send_v.at[block_of(s, target)],
             modes.at[pl.ds(c * MODES, MODES)],
@@ -202,7 +230,7 @@
         )
 
     def field_copy(d):
-        target = lax.rem(c + d, GROUPS)
+        target = in_peer(c, d)
         return pltpu.make_async_remote_copy(
             send_k.at[block_of(s, target)],
             fields.at[c],
@@ -222,6 +250,7 @@
     ]
 
     def send_faces_up():
+        loads[1].wait()
         loads[2].wait()
         for copy in z_copies:
             copy.start()
@@ -236,8 +265,6 @@
             modes[c * MODES + i] = send_v[block, i]
 
     def pack_fields():
-        loads[1].wait()
-
         @pl.loop(0, FIELDS * 3, unroll=4)
         def _(q):
             k, dim = lax.div(q, 3), lax.rem(q, 3)
@@ -295,7 +322,7 @@
         return copies
 
     def arrival(d):
-        return lax.rem(c + GROUPS - d, GROUPS)
+        return in_source(c, d)
 
     def forward(group):
         @pl.loop(0, MODES // 2, unroll=True)
@@ -403,18 +430,18 @@
     def all_differences(first, last):
         pl.loop(first, last)(differences)
 
+    pl.semaphore_wait(barrier, len(peers))
+    send_modes()
+    own_modes()
+    forward(c)
+    send_faces_up()
     pack_fields()
-    own_modes()
     tables()
-    pl.semaphore_wait(barrier, len(peers))
-    send_faces_up()
-    send_modes()
-    forward(c)
+    forward_arrivals(1, GROUPS)
     pack_faces_below()
+    send_fields()
     own_fields()
     mean_faces()
-    forward_arrivals(1, GROUPS)
-    send_fields()
     faces(c)
     all_differences(0, GROUPS)
     arrived_faces(1, GROUPS)

time: 37.8 us -> 36.9 us (0.976)
  Pallas kernels: 37.6 us -> 36.4 us
    pallas_call x1, Pallas kernels: 35.7 us -> 34.4 us  [shards(): pl.pallas_call(kernel, out_shape=jax.ShapeDtypeStruct((GROUPS, MODES) + t...]
where the time goes in v4:
time: 36.9 us; the launch traced here: 36.4 us
  Pallas kernels  36.4 us (99%)
    pallas_call x1, Pallas kernels, shards(): pl.pallas_call(kernel, out_shape=jax.ShapeDtypeStruct((GROUPS, MODES) + t...  34.4 us
    pallas_call x1, Pallas kernels, shards(): pl.pallas_call(unpack, out_shape=jax.ShapeDtypeStruct((MODES, 2, 32, 128)...  1.96 us

profile of v4, /device:TPU:32, one launch (start us, length us, event | category | flops | bytes accessed | tf_op | source)
XLA Modules:
  0.0 36.4 jit_solution(15689228166371531048)
XLA Ops:
  0.0 34.4 %apply.1.blocks_ref = f32[8,16,8,128]{3,2,1,0:T(8,128)} custom-call(f32[16,2,32,128]{3,2,1,0:T(8,128)} %sol_ref.1, f32[3,2,32,128]{3,2,1,0:T(8,128)} %mean_ref.1, f32[4,3,2,32,128]{4,3,2,1,0:T(8,128)} %kl_ref.1, s32[32,128]{1,0:T(8,128)} %bitcast.1), custom_call_target="tpu_custom_call" | custom-call | tf_op jit(solution)/shard_map/apply/pallas_call | solution.py:557
  34.4 2.0 %unpack.1 = f32[16,2,32,128]{3,2,1,0:T(8,128)} custom-call(f32[8,16,8,128]{3,2,1,0:T(8,128)} %apply.1.blocks_ref), custom_call_target="tpu_custom_call" | custom-call | tf_op jit(solution)/shard_map/unpack/pallas_call | solution.py:602

commit v5 on v4

--- a/solution.py
+++ b/solution.py
@@ -481,6 +481,17 @@
         level_b, flux_b = term(planes(face, b), planes(diff, 1 + a))
         result[p] = result[p] + weight * gather(level_a + level_b, flux_a + flux_b)
 
+    def pair_group(target):
+        @pl.loop(0, MODES, unroll=True)
+        def _(i):
+            pair(target * MODES + i)
+
+        send_result(target)
+
+    high = lax.div(c, 4)
+    early = (1 - high) * (4 + lax.rem(lax.rem(c, 4) + 2, 4)) + high * 3
+    pair_group(early)
+
     pl.loop(FIRST_PAIR, TOTAL, unroll=IMAGE_UNROLL)(image)
 
     zero = jnp.zeros((8, 128), F32)
@@ -517,13 +528,13 @@
     def _(d):
         target = out_peer(c, d)
 
-        @pl.when(target >= FULL_GROUP)
+        @pl.when((target >= FULL_GROUP) & (target != early))
         def _():
-            @pl.loop(0, MODES, unroll=True)
-            def _(i):
-                pair(target * MODES + i)
-
-        send_result(target)
+            pair_group(target)
+
+        @pl.when(target < FULL_GROUP)
+        def _():
+            send_result(target)
 
     for b in range(GROUPS):
         pltpu.make_async_copy(result.at[pl.ds(0, MODES)], out_ref.at[b], or_sem.at[b]).wait()
@@ -541,14 +552,23 @@
         pl.when(has_prev)(copies[3].wait_send)
 
 
-def unpack(blocks_ref, out_ref):
-    @pl.loop(0, MODES)
-    def _(i):
-        for t in range(4):
-            rows = pl.ds(8 * t, 8)
-            low, high = halves(blocks_ref[2 * t, i], blocks_ref[2 * t + 1, i])
-            out_ref[i, 0, rows, :] = low
-            out_ref[i, 1, rows, :] = high
+def unpack(blocks_ref, out_ref, landed, final, in_sem, out_sem):
+    loads, stores = [], []
+    for t in range(4):
+        part = pl.ds(2 * t, 2)
+        loads.append(pltpu.make_async_copy(blocks_ref.at[part], landed.at[part], in_sem.at[t]))
+        loads[-1].start()
+    for t in range(4):
+        rows = pl.ds(8 * t, 8)
+        loads[t].wait()
+        for i in range(MODES):
+            low, high = halves(landed[2 * t, i], landed[2 * t + 1, i])
+            final[i, 0, rows, :] = low
+            final[i, 1, rows, :] = high
+        stores.append(pltpu.make_async_copy(final.at[:, :, rows], out_ref.at[:, :, rows], out_sem.at[t]))
+        stores[-1].start()
+    for store in stores:
+        store.wait()
 
 
 def shards(sol, mean, kl, multi_index, couplings):
@@ -602,8 +622,15 @@
     return pl.pallas_call(
         unpack,
         out_shape=jax.ShapeDtypeStruct((MODES, 2, 32, 128), F32),
-        in_specs=[pl.BlockSpec(memory_space=pltpu.VMEM)],
-        out_specs=pl.BlockSpec(memory_space=pltpu.VMEM),
+        in_specs=[pl.BlockSpec(memory_space=pl.ANY)],
+        out_specs=pl.BlockSpec(memory_space=pl.ANY),
+        scratch_shapes=[
+            pltpu.VMEM((GROUPS, MODES) + tile, F32),
+            pltpu.VMEM((MODES, 2, 32, 128), F32),
+            sem((4,)),
+            sem((4,)),
+        ],
+        compiler_params=pltpu.CompilerParams(vmem_limit_bytes=60 * 2**20),
         name="unpack",
     )(blocks)
 

time: 36.9 us -> 36.6 us (level)
  no operation moved by 1% of the time
where the time goes in v5:
time: 36.6 us; the launch traced here: 36.4 us
  Pallas kernels  36.4 us (99%)
    pallas_call x1, Pallas kernels, shards(): pl.pallas_call(kernel, out_shape=jax.ShapeDtypeStruct((GROUPS, MODES) + t...  34.6 us
    pallas_call x1, Pallas kernels, shards(): pl.pallas_call(unpack, out_shape=jax.ShapeDtypeStruct((MODES, 2, 32, 128)...  1.84 us

profile of v5, /device:TPU:32, one launch (start us, length us, event | category | flops | bytes accessed | tf_op | source)
XLA Modules:
  0.0 36.4 jit_solution(1058021188983668488)
XLA Ops:
  0.0 34.6 %apply.1.blocks_ref = f32[8,16,8,128]{3,2,1,0:T(8,128)} custom-call(f32[16,2,32,128]{3,2,1,0:T(8,128)} %sol_ref.1, f32[3,2,32,128]{3,2,1,0:T(8,128)} %mean_ref.1, f32[4,3,2,32,128]{4,3,2,1,0:T(8,128)} %kl_ref.1, s32[32,128]{1,0:T(8,128)} %bitcast.1), custom_call_target="tpu_custom_call" | custom-call | tf_op jit(solution)/shard_map/apply/pallas_call | solution.py:577
  34.6 1.8 %unpack.1 = f32[16,2,32,128]{3,2,1,0:T(8,128)} custom-call(f32[8,16,8,128]{3,2,1,0:T(8,128)} %apply.1.blocks_ref), custom_call_target="tpu_custom_call" | custom-call | tf_op jit(solution)/shard_map/unpack/pallas_call | solution.py:622

commit v6 on v5

--- a/solution.py
+++ b/solution.py
@@ -64,6 +64,20 @@
     move = move + jnp.where(d == 5, 4, 0)
     move = move + jnp.where(d == 6, 1, 0)
     move = move + jnp.where(d == 7, 3, 0)
+    high = lax.rem(lax.div(chaos, 4) + lax.div(move, 4), 2)
+    return high * 4 + lax.rem(lax.rem(chaos, 4) + lax.rem(move, 4), 4)
+
+
+def field_peer(chaos, d):
+    d = lax.rem(d, 8)
+    move = d * 0
+    move = move + jnp.where(d == 1, 2, 0)
+    move = move + jnp.where(d == 2, 6, 0)
+    move = move + jnp.where(d == 3, 1, 0)
+    move = move + jnp.where(d == 4, 5, 0)
+    move = move + jnp.where(d == 5, 3, 0)
+    move = move + jnp.where(d == 6, 7, 0)
+    move = move + jnp.where(d == 7, 4, 0)
     high = lax.rem(lax.div(chaos, 4) + lax.div(move, 4), 2)
     return high * 4 + lax.rem(lax.rem(chaos, 4) + lax.rem(move, 4), 4)
 
@@ -230,7 +244,7 @@
         )
 
     def field_copy(d):
-        target = in_peer(c, d)
+        target = field_peer(c, d)
         return pltpu.make_async_remote_copy(
             send_k.at[block_of(s, target)],
             fields.at[c],
@@ -440,8 +454,8 @@
     forward_arrivals(1, GROUPS)
     pack_faces_below()
     send_fields()
+    mean_faces()
     own_fields()
-    mean_faces()
     faces(c)
     all_differences(0, GROUPS)
     arrived_faces(1, GROUPS)

time: 36.6 us -> 36.6 us (level)
  no operation moved by 1% of the time
where the time goes in v6:
time: 36.6 us; the launch traced here: 36.4 us
  Pallas kernels  36.4 us (99%)
    pallas_call x1, Pallas kernels, shards(): pl.pallas_call(kernel, out_shape=jax.ShapeDtypeStruct((GROUPS, MODES) + t...  34.6 us
    pallas_call x1, Pallas kernels, shards(): pl.pallas_call(unpack, out_shape=jax.ShapeDtypeStruct((MODES, 2, 32, 128)...  1.84 us

profile of v6, /device:TPU:32, one launch (start us, length us, event | category | flops | bytes accessed | tf_op | source)
XLA Modules:
  0.0 36.4 jit_solution(10863208079850973889)
XLA Ops:
  0.0 34.6 %apply.1.blocks_ref = f32[8,16,8,128]{3,2,1,0:T(8,128)} custom-call(f32[16,2,32,128]{3,2,1,0:T(8,128)} %sol_ref.1, f32[3,2,32,128]{3,2,1,0:T(8,128)} %mean_ref.1, f32[4,3,2,32,128]{4,3,2,1,0:T(8,128)} %kl_ref.1, s32[32,128]{1,0:T(8,128)} %bitcast.1), custom_call_target="tpu_custom_call" | custom-call | tf_op jit(solution)/shard_map/apply/pallas_call | solution.py:591
  34.6 1.8 %unpack.1 = f32[16,2,32,128]{3,2,1,0:T(8,128)} custom-call(f32[8,16,8,128]{3,2,1,0:T(8,128)} %apply.1.blocks_ref), custom_call_target="tpu_custom_call" | custom-call | tf_op jit(solution)/shard_map/unpack/pallas_call | solution.py:636
